TPU v7x, 768 devices: a whole 4x8x12 slice. The times are simulated.
768 devices in a mesh: blk: 384 (over x, z, y), grp: 2 (over core).
Axes of the slice: x: 4, y: 8, z: 12, core: 2. Of those that a mesh axis runs over, the one named last changes fastest.
Arguments:
- picture_embeddings: bfloat16 [98304, 1152], P('blk', 'grp')
- description_embeddings: bfloat16 [98304, 1152], P('blk', 'grp')
- sharpness_factor: float32 [1], replicated, may hold values from 10 to 30
- offset_term: float32 [1], replicated, may hold values from -3 to -1
Outputs:
- grad_image: float32 [98304, 1152], P('blk', 'grp')
- grad_text: float32 [98304, 1152], P('blk', 'grp')
All inputs are finite; a program needn't handle non-finite values.
Results may differ from a plain program's by a relative error of at most 0.0024.
Values may be sent and summed in bfloat16 or wider, within the bound.
A program may use at most 32 MiB of HBM per device.

v0:
```python
import jax
import jax.numpy as jnp
from jax import lax
from jax.sharding import PartitionSpec as P

HOPS = 8


def from_behind(value, axis, by):
    length = lax.axis_size(axis)
    return lax.ppermute(value, axis, [(i, (i + by) % length) for i in range(length)])


def on_device(picture_embeddings, description_embeddings, sharpness_factor, offset_term):
    similarity_multiplier = sharpness_factor[0]
    offset = offset_term[0]
    rows = picture_embeddings.shape[0]
    contract_dims = (((1,), (1,)), ((), ()))
    reduce_leading_axes = (((0,), (0,)), ((), ()))
    identity_matches = (
        jnp.arange(rows, dtype=jnp.int32)[:, None] == jnp.arange(rows, dtype=jnp.int32)[None, :]
    ).astype(jnp.float32)
    held = description_embeddings
    held_grad = jnp.zeros(description_embeddings.shape, jnp.float32)
    grad_image = jnp.zeros(picture_embeddings.shape, jnp.float32)
    for step in range(HOPS):
        partial_value = lax.dot_general(
            picture_embeddings, held, contract_dims, preferred_element_type=jnp.float32
        )
        dots = lax.psum(partial_value, "grp")
        probs = jax.nn.sigmoid(similarity_multiplier * dots + offset)
        if step == 0:
            probs = probs - identity_matches
        pair_coefficient = (similarity_multiplier * probs).astype(jnp.bfloat16)
        grad_image = grad_image + jnp.dot(
            pair_coefficient, held, preferred_element_type=jnp.float32
        )
        held_grad = held_grad + lax.dot_general(
            pair_coefficient,
            picture_embeddings,
            reduce_leading_axes,
            preferred_element_type=jnp.float32,
        )
        if step + 1 < HOPS:
            held = from_behind(held, "blk", 1)
            held_grad = from_behind(held_grad, "blk", 1)
    grad_text = from_behind(held_grad, "blk", 1 - HOPS)
    return (grad_image, grad_text)


def solution(mesh):
    placed = (P("blk", "grp"), P("blk", "grp"), P(), P())
    return jax.shard_map(
        on_device,
        mesh=mesh,
        in_specs=placed,
        out_specs=(P("blk", "grp"), P("blk", "grp")),
        check_vma=False,
    )
```

profile of v0, /device:TPU:1, one launch (start us, length us, event | category | flops | bytes accessed | tf_op | source)
XLA Modules:
  0.0 312.0 jit_solution(13512725487075394033)
XLA Ops:
  7.2 0.0 all-reduce.3.cloned.1.call-start
  7.2 4.2 %collective-permute-start = (bf16[256,576]{0,1:T(8,128)(2,1)}, bf16[256,576]{0,1:T(8,128)(2,1)S(1)}, u32[]{:S(2)}, u32[]{:S(2)}) collective-permute-start(bf16[256,576]{0,1:T(8,128)(2,1)} %param.5), channel_id=1, source_target_pairs={{0,2},{2,4},{4,6},{6,8},{8,10},{10,12},{12,14},{14,16},{16,18},{18... | collective-permute-start | bytes 884744 | tf_op jit(solution)/shard_map/ppermute | solution.py:11
  11.4 23.1 %collective-permute-done = bf16[256,576]{0,1:T(8,128)(2,1)S(1)} collective-permute-done((bf16[256,576]{0,1:T(8,128)(2,1)}, bf16[256,576]{0,1:T(8,128)(2,1)S(1)}, u32[]{:S(2)}, u32[]{:S(2)}) %collective-permute-start) | collective-permute-done | bytes 294944 | tf_op jit(solution)/shard_map/ppermute | solution.py:11
  34.5 1.9 collective-permute-start.1
  36.4 12.7 %collective-permute-done.1 = bf16[256,576]{0,1:T(8,128)(2,1)S(1)} collective-permute-done((bf16[256,576]{0,1:T(8,128)(2,1)S(1)}, bf16[256,576]{0,1:T(8,128)(2,1)S(1)}, u32[]{:S(2)}, u32[]{:S(2)}) %collective-permute-start.1) | collective-permute-done | bytes 294944 | tf_op jit(solution)/shard_map/ppermute | solution.py:11
  49.1 1.9 collective-permute-start.2
  51.0 11.7 %collective-permute-done.2 = bf16[256,576]{0,1:T(8,128)(2,1)S(1)} collective-permute-done((bf16[256,576]{0,1:T(8,128)(2,1)S(1)}, bf16[256,576]{0,1:T(8,128)(2,1)S(1)}, u32[]{:S(2)}, u32[]{:S(2)}) %collective-permute-start.2) | collective-permute-done | bytes 294944 | tf_op jit(solution)/shard_map/ppermute | solution.py:11
  62.8 1.9 collective-permute-start.3
  64.7 2.0 fusion.8
  66.7 9.0 %collective-permute-done.3 = bf16[256,576]{0,1:T(8,128)(2,1)S(1)} collective-permute-done((bf16[256,576]{0,1:T(8,128)(2,1)S(1)}, bf16[256,576]{0,1:T(8,128)(2,1)S(1)}, u32[]{:S(2)}, u32[]{:S(2)}) %collective-permute-start.3) | collective-permute-done | bytes 294944 | tf_op jit(solution)/shard_map/ppermute | solution.py:11
  75.7 1.9 collective-permute-start.4
  77.6 1.0 fusion.9
  78.6 1.0 fusion.10
  79.6 9.0 %collective-permute-done.4 = bf16[256,576]{0,1:T(8,128)(2,1)S(1)} collective-permute-done((bf16[256,576]{0,1:T(8,128)(2,1)S(1)}, bf16[256,576]{0,1:T(8,128)(2,1)S(1)}, u32[]{:S(2)}, u32[]{:S(2)}) %collective-permute-start.4) | collective-permute-done | bytes 294944 | tf_op jit(solution)/shard_map/ppermute | solution.py:11
  88.5 1.9 collective-permute-start.5
  90.5 1.0 fusion.11
  91.5 1.0 fusion.12
  92.5 8.9 %collective-permute-done.5 = bf16[256,576]{0,1:T(8,128)(2,1)S(1)} collective-permute-done((bf16[256,576]{0,1:T(8,128)(2,1)S(1)}, bf16[256,576]{0,1:T(8,128)(2,1)S(1)}, u32[]{:S(2)}, u32[]{:S(2)}) %collective-permute-start.5) | collective-permute-done | bytes 294944 | tf_op jit(solution)/shard_map/ppermute | solution.py:11
  101.4 1.9 collective-permute-start.6
  103.4 1.0 fusion.13
  104.4 1.0 fusion.14
  105.4 8.9 %collective-permute-done.6 = bf16[256,576]{0,1:T(8,128)(2,1)S(1)} collective-permute-done((bf16[256,576]{0,1:T(8,128)(2,1)S(1)}, bf16[256,576]{0,1:T(8,128)(2,1)S(1)}, u32[]{:S(2)}, u32[]{:S(2)}) %collective-permute-start.6) | collective-permute-done | bytes 294944 | tf_op jit(solution)/shard_map/ppermute | solution.py:11
  114.3 1.0 fusion.15
  116.6 36.9 %all-reduce.3.cloned.1.call-done = (f32[256,256]{1,0:T(8,128)}, f32[256,256]{1,0:T(8,128)}, f32[256,256]{1,0:T(8,128)}, f32[256,256]{1,0:T(8,128)}, f32[256,256]...) async-done(((f32[256,256]{1,0:T(8,128)}, f32[256,256]{1,0:T(8,128)}, f32[256,256]{1,0:T(8,128)}, f32[256,256]{1,0:T(8,128)}, ...) | async-done | bytes 2097168 | tf_op jit(solution)/shard_map/psum | solution.py:30
  153.5 1.3 fusion.6
  154.8 1.9 collective-permute-start.7
  156.8 20.5 %collective-permute-done.7 = f32[256,576]{0,1:T(8,128)S(1)} collective-permute-done((f32[256,576]{0,1:T(8,128)S(1)}, f32[256,576]{0,1:T(8,128)S(1)}, u32[]{:S(2)}, u32[]{:S(2)}) %collective-permute-start.7) | collective-permute-done | bytes 589856 | tf_op jit(solution)/shard_map/ppermute | solution.py:11
  177.3 0.3 convolution_add_fusion
  177.6 1.9 collective-permute-start.8
  179.5 0.3 fusion
  179.8 19.2 %collective-permute-done.8 = f32[256,576]{0,1:T(8,128)S(1)} collective-permute-done((f32[256,576]{0,1:T(8,128)S(1)}, f32[256,576]{0,1:T(8,128)S(1)}, u32[]{:S(2)}, u32[]{:S(2)}) %collective-permute-start.8) | collective-permute-done | bytes 589856 | tf_op jit(solution)/shard_map/ppermute | solution.py:11
  198.9 0.1 add.141
  199.0 1.9 collective-permute-start.9
  201.0 0.3 fusion.1
  201.3 18.2 %collective-permute-done.9 = f32[256,576]{0,1:T(8,128)S(1)} collective-permute-done((f32[256,576]{0,1:T(8,128)S(1)}, f32[256,576]{0,1:T(8,128)S(1)}, u32[]{:S(2)}, u32[]{:S(2)}) %collective-permute-start.9) | collective-permute-done | bytes 589856 | tf_op jit(solution)/shard_map/ppermute | solution.py:11
  219.5 0.1 add.142
  219.6 1.9 collective-permute-start.10
  221.5 0.3 fusion.2
  221.8 17.3 %collective-permute-done.10 = f32[256,576]{0,1:T(8,128)S(1)} collective-permute-done((f32[256,576]{0,1:T(8,128)S(1)}, f32[256,576]{0,1:T(8,128)S(1)}, u32[]{:S(2)}, u32[]{:S(2)}) %collective-permute-start.10) | collective-permute-done | bytes 589856 | tf_op jit(solution)/shard_map/ppermute | solution.py:11
  239.1 0.1 add.143
  239.2 1.9 collective-permute-start.11
  241.1 0.3 fusion.7
  241.4 0.6 copy-done.5
  242.1 0.3 fusion.3
  242.4 15.4 %collective-permute-done.11 = f32[256,576]{0,1:T(8,128)S(1)} collective-permute-done((f32[256,576]{0,1:T(8,128)S(1)}, f32[256,576]{0,1:T(8,128)S(1)}, u32[]{:S(2)}, u32[]{:S(2)}) %collective-permute-start.11) | collective-permute-done | bytes 589856 | tf_op jit(solution)/shard_map/ppermute | solution.py:11
  257.8 0.1 add.144
  257.9 1.9 collective-permute-start.12
  259.8 0.3 fusion.4
  260.1 0.3 convolution_add_fusion.7
  260.4 0.3 convolution_add_fusion.6
  260.7 14.9 %collective-permute-done.12 = f32[256,576]{0,1:T(8,128)S(1)} collective-permute-done((f32[256,576]{0,1:T(8,128)S(1)}, f32[256,576]{0,1:T(8,128)S(1)}, u32[]{:S(2)}, u32[]{:S(2)}) %collective-permute-start.12) | collective-permute-done | bytes 589856 | tf_op jit(solution)/shard_map/ppermute | solution.py:11
  275.6 0.1 add.145
  275.6 1.9 collective-permute-start.13
  277.6 0.3 fusion.5
  277.9 0.3 convolution_add_fusion.5
  278.2 0.3 convolution_add_fusion.4
  278.5 14.0 %collective-permute-done.13 = f32[256,576]{0,1:T(8,128)S(1)} collective-permute-done((f32[256,576]{0,1:T(8,128)S(1)}, f32[256,576]{0,1:T(8,128)S(1)}, u32[]{:S(2)}, u32[]{:S(2)}) %collective-permute-start.13) | collective-permute-done | bytes 589856 | tf_op jit(solution)/shard_map/ppermute | solution.py:11
  292.4 0.1 add.146
  292.5 1.9 collective-permute-start.14
  294.4 0.3 convolution_add_fusion.3
  294.7 0.3 convolution_add_fusion.2
  295.0 1.1 convolution_add_fusion.1
  296.1 8.2 %collective-permute-done.14 = f32[256,576]{0,1:T(8,128)S(1)} collective-permute-done((f32[256,576]{0,1:T(8,128)S(1)}, f32[256,576]{0,1:T(8,128)S(1)}, u32[]{:S(2)}, u32[]{:S(2)}) %collective-permute-start.14) | collective-permute-done | bytes 589856 | tf_op jit(solution)/shard_map/ppermute | solution.py:11
  304.3 0.8 copy.17
  (20 shorter events, 0.1 us)
Async XLA Ops:
  7.2 57.5 %copy-start = (bf16[256,576]{0,1:T(8,128)(2,1)S(1)}, bf16[256,576]{0,1:T(8,128)(2,1)}, u32[]{:S(2)}) copy-start(bf16[256,576]{0,1:T(8,128)(2,1)} %param.4) | copy-start | bytes 884740
  7.2 146.4 %all-reduce.3.cloned.1.call-start = ((), (), s32[]{:S(2)}) async-start(), calls=%async_computation | async-start | bytes 4194304 | tf_op jit(solution)/shard_map/psum | solution.py:30
  7.2 27.3 %collective-permute-start = (bf16[256,576]{0,1:T(8,128)(2,1)}, bf16[256,576]{0,1:T(8,128)(2,1)S(1)}, u32[]{:S(2)}, u32[]{:S(2)}) collective-permute-start(bf16[256,576]{0,1:T(8,128)(2,1)} %param.5), channel_id=1, source_target_pairs={{0,2},{2,4},{4,6},{6,8},{8,10},{10,12},{12,14},{14,16},{16,18},{18... | collective-permute-start | bytes 884744 | tf_op jit(solution)/shard_map/ppermute | solution.py:11
  34.5 14.6 %collective-permute-start.1 = (bf16[256,576]{0,1:T(8,128)(2,1)S(1)}, bf16[256,576]{0,1:T(8,128)(2,1)S(1)}, u32[]{:S(2)}, u32[]{:S(2)}) collective-permute-start(bf16[256,576]{0,1:T(8,128)(2,1)S(1)} %collective-permute-done), channel_id=1, source_target_pairs={{0,2},{2,4},{4,6},{6,8},{8,10},{10,12},{12,14},{14,16},{16,18},{18... | collective-permute-start | bytes 884744 | tf_op jit(solution)/shard_map/ppermute | solution.py:11
  49.1 13.7 %collective-permute-start.2 = (bf16[256,576]{0,1:T(8,128)(2,1)S(1)}, bf16[256,576]{0,1:T(8,128)(2,1)S(1)}, u32[]{:S(2)}, u32[]{:S(2)}) collective-permute-start(bf16[256,576]{0,1:T(8,128)(2,1)S(1)} %collective-permute-done.1), channel_id=1, source_target_pairs={{0,2},{2,4},{4,6},{6,8},{8,10},{10,12},{12,14},{14,16},{16,18},{18... | collective-permute-start | bytes 884744 | tf_op jit(solution)/shard_map/ppermute | solution.py:11
  62.8 12.9 %collective-permute-start.3 = (bf16[256,576]{0,1:T(8,128)(2,1)S(1)}, bf16[256,576]{0,1:T(8,128)(2,1)S(1)}, u32[]{:S(2)}, u32[]{:S(2)}) collective-permute-start(bf16[256,576]{0,1:T(8,128)(2,1)S(1)} %collective-permute-done.2), channel_id=1, source_target_pairs={{0,2},{2,4},{4,6},{6,8},{8,10},{10,12},{12,14},{14,16},{16,18},{18... | collective-permute-start | bytes 884744 | tf_op jit(solution)/shard_map/ppermute | solution.py:11
  75.7 12.9 %collective-permute-start.4 = (bf16[256,576]{0,1:T(8,128)(2,1)S(1)}, bf16[256,576]{0,1:T(8,128)(2,1)S(1)}, u32[]{:S(2)}, u32[]{:S(2)}) collective-permute-start(bf16[256,576]{0,1:T(8,128)(2,1)S(1)} %collective-permute-done.3), channel_id=1, source_target_pairs={{0,2},{2,4},{4,6},{6,8},{8,10},{10,12},{12,14},{14,16},{16,18},{18... | collective-permute-start | bytes 884744 | tf_op jit(solution)/shard_map/ppermute | solution.py:11
  88.5 12.9 %collective-permute-start.5 = (bf16[256,576]{0,1:T(8,128)(2,1)S(1)}, bf16[256,576]{0,1:T(8,128)(2,1)S(1)}, u32[]{:S(2)}, u32[]{:S(2)}) collective-permute-start(bf16[256,576]{0,1:T(8,128)(2,1)S(1)} %collective-permute-done.4), channel_id=1, source_target_pairs={{0,2},{2,4},{4,6},{6,8},{8,10},{10,12},{12,14},{14,16},{16,18},{18... | collective-permute-start | bytes 884744 | tf_op jit(solution)/shard_map/ppermute | solution.py:11
  101.4 12.9 %collective-permute-start.6 = (bf16[256,576]{0,1:T(8,128)(2,1)S(1)}, bf16[256,576]{0,1:T(8,128)(2,1)S(1)}, u32[]{:S(2)}, u32[]{:S(2)}) collective-permute-start(bf16[256,576]{0,1:T(8,128)(2,1)S(1)} %collective-permute-done.5), channel_id=1, source_target_pairs={{0,2},{2,4},{4,6},{6,8},{8,10},{10,12},{12,14},{14,16},{16,18},{18... | collective-permute-start | bytes 884744 | tf_op jit(solution)/shard_map/ppermute | solution.py:11
  153.5 23.8 %copy-start.1 = (f32[256,256]{1,0:T(8,128)S(1)}, f32[256,256]{1,0:T(8,128)}, u32[]{:S(2)}) copy-start(f32[256,256]{1,0:T(8,128)} %get-tuple-element.3) | copy-start | bytes 786436
  154.8 22.5 %collective-permute-start.7 = (f32[256,576]{0,1:T(8,128)S(1)}, f32[256,576]{0,1:T(8,128)S(1)}, u32[]{:S(2)}, u32[]{:S(2)}) collective-permute-start(f32[256,576]{0,1:T(8,128)S(1)} %fusion.6), channel_id=1, source_target_pairs={{0,2},{2,4},{4,6},{6,8},{8,10},{10,12},{12,14},{14,16},{16,18},{18... | collective-permute-start | bytes 1769480 | tf_op jit(solution)/shard_map/ppermute | solution.py:11
  177.3 2.2 copy-start.8
  177.6 21.4 %collective-permute-start.8 = (f32[256,576]{0,1:T(8,128)S(1)}, f32[256,576]{0,1:T(8,128)S(1)}, u32[]{:S(2)}, u32[]{:S(2)}) collective-permute-start(f32[256,576]{0,1:T(8,128)S(1)} %convolution_add_fusion), channel_id=1, source_target_pairs={{0,2},{2,4},{4,6},{6,8},{8,10},{10,12},{12,14},{14,16},{16,18},{18... | collective-permute-start | bytes 1769480 | tf_op jit(solution)/shard_map/ppermute | solution.py:11
  179.8 21.2 %copy-start.7 = (f32[256,256]{1,0:T(8,128)S(1)}, f32[256,256]{1,0:T(8,128)}, u32[]{:S(2)}) copy-start(f32[256,256]{1,0:T(8,128)} %get-tuple-element.5) | copy-start | bytes 786436
  199.0 20.5 %collective-permute-start.9 = (f32[256,576]{0,1:T(8,128)S(1)}, f32[256,576]{0,1:T(8,128)S(1)}, u32[]{:S(2)}, u32[]{:S(2)}) collective-permute-start(f32[256,576]{0,1:T(8,128)S(1)} %add.141), channel_id=1, source_target_pairs={{0,2},{2,4},{4,6},{6,8},{8,10},{10,12},{12,14},{14,16},{16,18},{18... | collective-permute-start | bytes 1769480 | tf_op jit(solution)/shard_map/ppermute | solution.py:11
  201.2 20.2 %copy-start.6 = (f32[256,256]{1,0:T(8,128)S(1)}, f32[256,256]{1,0:T(8,128)}, u32[]{:S(2)}) copy-start(f32[256,256]{1,0:T(8,128)} %get-tuple-element.6) | copy-start | bytes 786436
  219.6 19.5 %collective-permute-start.10 = (f32[256,576]{0,1:T(8,128)S(1)}, f32[256,576]{0,1:T(8,128)S(1)}, u32[]{:S(2)}, u32[]{:S(2)}) collective-permute-start(f32[256,576]{0,1:T(8,128)S(1)} %add.142), channel_id=1, source_target_pairs={{0,2},{2,4},{4,6},{6,8},{8,10},{10,12},{12,14},{14,16},{16,18},{18... | collective-permute-start | bytes 1769480 | tf_op jit(solution)/shard_map/ppermute | solution.py:11
  221.8 19.3 %copy-start.2 = (bf16[256,576]{0,1:T(8,128)(2,1)S(1)}, bf16[256,576]{0,1:T(8,128)(2,1)}, u32[]{:S(2)}) copy-start(bf16[256,576]{0,1:T(8,128)(2,1)} %param.5) | copy-start | bytes 884740
  221.8 19.3 %copy-start.9 = (f32[256,256]{1,0:T(8,128)S(1)}, f32[256,256]{1,0:T(8,128)}, u32[]{:S(2)}) copy-start(f32[256,256]{1,0:T(8,128)} %get-tuple-element.2) | copy-start | bytes 786436
  239.2 18.6 %collective-permute-start.11 = (f32[256,576]{0,1:T(8,128)S(1)}, f32[256,576]{0,1:T(8,128)S(1)}, u32[]{:S(2)}, u32[]{:S(2)}) collective-permute-start(f32[256,576]{0,1:T(8,128)S(1)} %add.143), channel_id=1, source_target_pairs={{0,2},{2,4},{4,6},{6,8},{8,10},{10,12},{12,14},{14,16},{16,18},{18... | collective-permute-start | bytes 1769480 | tf_op jit(solution)/shard_map/ppermute | solution.py:11
  241.1 1.0 copy-start.5
  242.4 17.4 %copy-start.4 = (f32[256,256]{1,0:T(8,128)S(1)}, f32[256,256]{1,0:T(8,128)}, u32[]{:S(2)}) copy-start(f32[256,256]{1,0:T(8,128)} %get-tuple-element.8) | copy-start | bytes 786436
  257.9 17.7 %collective-permute-start.12 = (f32[256,576]{0,1:T(8,128)S(1)}, f32[256,576]{0,1:T(8,128)S(1)}, u32[]{:S(2)}, u32[]{:S(2)}) collective-permute-start(f32[256,576]{0,1:T(8,128)S(1)} %add.144), channel_id=1, source_target_pairs={{0,2},{2,4},{4,6},{6,8},{8,10},{10,12},{12,14},{14,16},{16,18},{18... | collective-permute-start | bytes 1769480 | tf_op jit(solution)/shard_map/ppermute | solution.py:11
  260.7 16.9 %copy-start.3 = (f32[256,256]{1,0:T(8,128)S(1)}, f32[256,256]{1,0:T(8,128)}, u32[]{:S(2)}) copy-start(f32[256,256]{1,0:T(8,128)} %get-tuple-element.9) | copy-start | bytes 786436
  275.6 16.8 %collective-permute-start.13 = (f32[256,576]{0,1:T(8,128)S(1)}, f32[256,576]{0,1:T(8,128)S(1)}, u32[]{:S(2)}, u32[]{:S(2)}) collective-permute-start(f32[256,576]{0,1:T(8,128)S(1)} %add.145), channel_id=1, source_target_pairs={{0,2},{2,4},{4,6},{6,8},{8,10},{10,12},{12,14},{14,16},{16,18},{18... | collective-permute-start | bytes 1769480 | tf_op jit(solution)/shard_map/ppermute | solution.py:11
  292.5 11.8 %collective-permute-start.14 = (f32[256,576]{0,1:T(8,128)S(1)}, f32[256,576]{0,1:T(8,128)S(1)}, u32[]{:S(2)}, u32[]{:S(2)}) collective-permute-start(f32[256,576]{0,1:T(8,128)S(1)} %add.146), channel_id=1, source_target_pairs={{0,754},{2,756},{4,758},{6,760},{8,762},{10,764},{12,766},{14,0},{... | collective-permute-start | bytes 1769480 | tf_op jit(solution)/shard_map/ppermute | solution.py:11
Sparse Core Ops, SparseCore 0:
  115.5 38.0 all-reduce.2
where the time goes:
time: 316 us; the launch traced here: 312 us
  waiting for transfers between devices  248 us (78%)
  starting transfers between devices  31 us (10%)
  between operations  15.7 us (5%)
  matrix products  15.3 us (5%)
    ppermute x15, waiting for transfers between devices, from_behind(): lax.ppermute(value, axis, [(i, (i + by) % length) for i in range(length)])  211 us
    psum x1, waiting for transfers between devices, on_device(): dots = lax.psum(partial_value, 'grp')  36.9 us
    ppermute x15, starting transfers between devices, from_behind(): lax.ppermute(value, axis, [(i, (i + by) % length) for i in range(length)])  31 us
    dot_general x8, matrix products, on_device(): lax.dot_general(picture_embeddings, held, contract_dims, preferred_elemen...  8.98 us
  transfers between devices with their start and end apart: 16, of which 16 were waited for; matrix products, arithmetic and copies ran while one was open for 4% of the time, Pallas kernels for 0%

commit v1 on v0

v1 whole, which is shorter than its diff:
```python
import functools

import jax
import jax.numpy as jnp
from jax import lax
from jax.experimental import pallas as pl
from jax.experimental.pallas import tpu as pltpu
from jax.sharding import PartitionSpec as P

HOPS = 8
PIECES = 4
SLOTS = 2 * HOPS
MESH = pl.DeviceIdType.MESH


def kernel(
    n,
    scale_ref,
    offset_ref,
    image_ref,
    text_ref,
    out_ref,
    blocks,
    own,
    sent,
    got,
    first_sem,
    send_sem,
    recv_sem,
    core_send_sem,
    core_recv_sem,
):
    me = lax.axis_index("blk")
    core = lax.axis_index("grp")
    width, rows = image_ref.shape
    piece = width // PIECES
    ahead, behind = lax.rem(me + 1, n), lax.rem(me + n - 1, n)
    far_ahead, far_behind = lax.rem(me + 7, n), lax.rem(me + n - 7, n)
    partner = (me, 1 - core)

    barrier = pltpu.get_barrier_semaphore()
    others = [(ahead, core), (behind, core), (far_ahead, core), (far_behind, core), partner]
    for other in others:
        pl.semaphore_signal(barrier, inc=1, device_id=other, device_id_type=MESH)
    pl.semaphore_wait(barrier, len(others))

    def part(j):
        return pl.ds(pl.multiple_of(j * piece, 16), piece)

    def first_copy(k, j):
        to = (ahead, behind, far_ahead, far_behind)[k]
        source = image_ref if k % 2 else text_ref
        return pltpu.make_async_remote_copy(
            src_ref=source.at[part(j)],
            dst_ref=blocks.at[2 + k, part(j)],
            send_sem=first_sem.at[k, j],
            recv_sem=recv_sem.at[2 + k, j],
            device_id=(to, core),
            device_id_type=MESH,
        )

    def next_copy(k, s, j):
        to = ahead if k in (0, 3) else behind
        t = 2 + 4 * s + k
        return pltpu.make_async_remote_copy(
            src_ref=blocks.at[t, part(j)],
            dst_ref=blocks.at[t + 4, part(j)],
            send_sem=send_sem.at[t, j],
            recv_sem=recv_sem.at[t + 4, j],
            device_id=(to, core),
            device_id_type=MESH,
        )

    def core_copy(t):
        return pltpu.make_async_remote_copy(
            src_ref=sent.at[t],
            dst_ref=got.at[t],
            send_sem=core_send_sem.at[t],
            recv_sem=core_recv_sem.at[t],
            device_id=partner,
            device_id_type=MESH,
        )

    for j in range(PIECES):
        for k in range(4):
            first_copy(k, j).start()

    blocks[0] = text_ref[...]
    blocks[1] = image_ref[...]
    own[0] = image_ref[...].T
    own[1] = text_ref[...].T
    scale, offset = scale_ref[0], offset_ref[0]

    def dots(t):
        sent[t] = jnp.dot(own[lax.rem(t, 2)], blocks[t], preferred_element_type=jnp.float32)
        core_copy(t).start()

    def grads(t, match):
        core_copy(t).wait()
        probs = jax.nn.sigmoid(scale * (sent[t] + got[t]) + offset)
        if match:
            row = lax.broadcasted_iota(jnp.int32, (rows, rows), 0)
            column = lax.broadcasted_iota(jnp.int32, (rows, rows), 1)
            probs = probs - (row == column).astype(jnp.float32)
        weight = (scale * probs).astype(jnp.bfloat16)
        term = lax.dot_general(
            blocks[t], weight, (((1,), (1,)), ((), ())), preferred_element_type=jnp.float32
        )
        side = lax.rem(t, 2)
        if match:
            out_ref[side] = term
        else:
            out_ref[side] = out_ref[side] + term

    dots(0)
    dots(1)
    grads(0, True)
    grads(1, True)

    @pl.loop(0, 4 * PIECES)
    def _(i):
        s, j = i // PIECES, lax.rem(i, PIECES)
        for k in range(4):

            @pl.when(s < (4 if k < 2 else 3))
            def _():
                t = 2 + 4 * s + k
                pltpu.make_async_remote_copy(
                    src_ref=blocks.at[t, part(j)],
                    dst_ref=blocks.at[t, part(j)],
                    send_sem=send_sem.at[t, j],
                    recv_sem=recv_sem.at[t, j],
                    device_id=(behind, core),
                    device_id_type=MESH,
                ).wait_recv()

            @pl.when(s < (3 if k < 2 else 2))
            def _():
                next_copy(k, s, j).start()

        @pl.when(s > 0)
        def _():
            t = i - PIECES + 2
            dots(t)

            @pl.when(t > 2)
            def _():
                grads(t - 1, False)

    dots(SLOTS - 2)
    grads(SLOTS - 3, False)
    dots(SLOTS - 1)
    grads(SLOTS - 2, False)
    grads(SLOTS - 1, False)

    for j in range(PIECES):
        for k in range(4):
            first_copy(k, j).wait_send()

    @pl.loop(0, 3 * PIECES)
    def _(i):
        s, j = i // PIECES, lax.rem(i, PIECES)
        for k in range(4):

            @pl.when(s < (3 if k < 2 else 2))
            def _():
                next_copy(k, s, j).wait_send()


def on_device(n, picture_embeddings, description_embeddings, sharpness_factor, offset_term):
    rows, width = picture_embeddings.shape
    vmem = pl.BlockSpec(memory_space=pltpu.VMEM)
    smem = pl.BlockSpec(memory_space=pltpu.SMEM)
    grads = pl.pallas_call(
        functools.partial(kernel, n),
        out_shape=jax.ShapeDtypeStruct((2, width, rows), jnp.float32),
        in_specs=[smem, smem, vmem, vmem],
        out_specs=vmem,
        scratch_shapes=[
            pltpu.VMEM((SLOTS, width, rows), jnp.bfloat16),
            pltpu.VMEM((2, rows, width), jnp.bfloat16),
            pltpu.VMEM((SLOTS, rows, rows), jnp.float32),
            pltpu.VMEM((SLOTS, rows, rows), jnp.float32),
            pltpu.SemaphoreType.DMA((4, PIECES)),
            pltpu.SemaphoreType.DMA((SLOTS, PIECES)),
            pltpu.SemaphoreType.DMA((SLOTS, PIECES)),
            pltpu.SemaphoreType.DMA((SLOTS,)),
            pltpu.SemaphoreType.DMA((SLOTS,)),
        ],
        compiler_params=pltpu.CompilerParams(
            collective_id=0, has_side_effects=True, vmem_limit_bytes=40 * 1024 * 1024
        ),
    )(sharpness_factor, offset_term, picture_embeddings.T, description_embeddings.T)
    return grads[0].T, grads[1].T


def solution(mesh):
    placed = (P("blk", "grp"), P("blk", "grp"), P(), P())
    return jax.shard_map(
        functools.partial(on_device, mesh.shape["blk"]),
        mesh=mesh,
        in_specs=placed,
        out_specs=(P("blk", "grp"), P("blk", "grp")),
        check_vma=False,
    )
```

time: 316 us -> 81.2 us (0.26)
  the two profiles are of different devices: /device:TPU:1 before, /device:TPU:65 now
where the time goes in v1:
time: 81.2 us; the launch traced here: 81 us
  Pallas kernels  76.1 us (94%)
  local copies, waits for them, and re-layouts  3 us (4%)
  between operations  1.94 us (2%)
    pallas_call x1, Pallas kernels, on_device(): pl.pallas_call(functools.partial(kernel, n), out_shape=jax.ShapeDtypeStru...  76.1 us
    unnamed x4, local copies, waits for them, and re-layouts  1.92 us

profile of v1, /device:TPU:65, one launch (start us, length us, event | category | flops | bytes accessed | tf_op | source)
XLA Modules:
  0.0 81.0 jit_solution(9121769361022658007)
XLA Ops:
  1.9 0.0 copy-start
  1.9 1.0 %copy-done = bf16[256,576]{0,1:T(8,128)(2,1)S(1)} copy-done((bf16[256,576]{0,1:T(8,128)(2,1)S(1)}, bf16[256,576]{0,1:T(8,128)(2,1)}, u32[]{:S(2)}) %copy-start) | copy-done | bytes 294936
  2.9 0.0 copy-start.1
  2.9 1.0 %copy-done.1 = bf16[256,576]{0,1:T(8,128)(2,1)S(1)} copy-done((bf16[256,576]{0,1:T(8,128)(2,1)S(1)}, bf16[256,576]{0,1:T(8,128)(2,1)}, u32[]{:S(2)}) %copy-start.1) | copy-done | bytes 294936
  3.8 76.1 %shard_map.59 = f32[2,576,256]{2,1,0:T(8,128)S(1)} custom-call(f32[1]{0:T(128)S(6)} %copy.6.scale_ref, f32[1]{0:T(128)S(6)} %copy.7.offset_ref, bf16[576,256]{1,0:T(8,128)(2,1)S(1)} %bitcast.10, bf16[576,256]{1,0:T(8,128)(2,1)S(1)} %bitcast.11), custom_call_target="tpu_custom_call" | custom-call | tf_op jit(solution)/shard_map/pallas_call | solution.py:174
  79.9 1.1 %slice_bitcast_fusion = (f32[256,576]{0,1:T(8,128)}, f32[256,576]{0,1:T(8,128)}) fusion(f32[2,576,256]{2,1,0:T(8,128)S(1)} %shard_map.59), kind=kLoop, calls=%fused_computation | loop fusion | bytes 2359296 | tf_op jit(solution)/shard_map/transpose | solution.py:194
Async XLA Ops:
  1.9 1.0 %copy-start = (bf16[256,576]{0,1:T(8,128)(2,1)S(1)}, bf16[256,576]{0,1:T(8,128)(2,1)}, u32[]{:S(2)}) copy-start(bf16[256,576]{0,1:T(8,128)(2,1)} %param.4) | copy-start | bytes 884740
  2.9 1.0 %copy-start.1 = (bf16[256,576]{0,1:T(8,128)(2,1)S(1)}, bf16[256,576]{0,1:T(8,128)(2,1)}, u32[]{:S(2)}) copy-start(bf16[256,576]{0,1:T(8,128)(2,1)} %param.5) | copy-start | bytes 884740

commit v2 on v1

v2 whole, which is shorter than its diff:
```python
import functools

import jax
import jax.numpy as jnp
from jax import lax
from jax.experimental import pallas as pl
from jax.experimental.pallas import tpu as pltpu
from jax.sharding import PartitionSpec as P

HOPS = 8
PIECES = 4
WINDOW = 4
DELAY = 4
LAG = 5
EACH = PIECES // 2
SLOTS = 2 * HOPS
STEPS = (HOPS - 1) * PIECES
MESH = pl.DeviceIdType.MESH


def kernel(
    n,
    scale_ref,
    offset_ref,
    image_ref,
    text_ref,
    out_ref,
    blocks,
    own,
    sent,
    got,
    load_sem,
    send_sem,
    recv_sem,
    row_send_sem,
    row_recv_sem,
    core_send_sem,
    core_recv_sem,
):
    me = lax.axis_index("blk")
    core = lax.axis_index("grp")
    width, rows = image_ref.shape
    piece = width // PIECES
    place = lax.rem(me, HOPS)
    start = me - place
    ahead = start + lax.rem(place + 1, HOPS)
    behind = start + lax.rem(place + HOPS - 1, HOPS)
    above, below = lax.rem(me + HOPS, n), lax.rem(me + n - HOPS, n)
    partner = (me, 1 - core)

    loads = [
        pltpu.make_async_copy(text_ref, blocks.at[0, 0], load_sem.at[0]),
        pltpu.make_async_copy(image_ref, blocks.at[0, 1], load_sem.at[1]),
    ]
    for load in loads:
        load.start()
    barrier = pltpu.get_barrier_semaphore()
    others = [(ahead, core), (behind, core), (above, core), (below, core), partner]
    for other in others:
        pl.semaphore_signal(barrier, inc=1, device_id=other, device_id_type=MESH)
    out_ref[...] = jnp.zeros_like(out_ref)
    for load in loads:
        load.wait()
    pl.semaphore_wait(barrier, len(others))

    def part(j):
        return pl.ds(pl.multiple_of(j * piece, 16), piece)

    def ring_copy(q, d):
        r, j = q // PIECES, lax.rem(q, PIECES)
        t = 2 + 2 * r + d
        return pltpu.make_async_remote_copy(
            src_ref=blocks.at[0, jnp.where(r < 2, lax.rem(r + d, 2), t - 4), part(j)],
            dst_ref=blocks.at[0, t, part(j)],
            send_sem=send_sem.at[d, lax.rem(q, WINDOW)],
            recv_sem=recv_sem.at[t, j],
            device_id=(behind if d else ahead, core),
            device_id_type=MESH,
        )

    def row_copy(t, where, to):
        return pltpu.make_async_remote_copy(
            src_ref=blocks.at[0, t, where],
            dst_ref=blocks.at[1, t, where],
            send_sem=row_send_sem.at[t],
            recv_sem=row_recv_sem.at[t],
            device_id=(to, core),
            device_id_type=MESH,
        )

    def elsewhere(t):
        r, d = t // 2 - 1, lax.rem(t, 2)
        s = r // 2
        wrapped = jnp.where(d == 0, place - 1 - s < 0, place + 1 + s >= HOPS)
        return (t >= 2) & (wrapped == (lax.rem(r, 2) == 0))

    def side(t):
        return jnp.where(t < 2, t, lax.rem(t // 2 + 1 + lax.rem(t, 2), 2))

    def core_copy(t):
        return pltpu.make_async_remote_copy(
            src_ref=sent.at[t],
            dst_ref=got.at[t],
            send_sem=core_send_sem.at[t],
            recv_sem=core_recv_sem.at[t],
            device_id=partner,
            device_id_type=MESH,
        )

    def arrive(q):
        r, j = q // PIECES, lax.rem(q, PIECES)
        for d in range(2):
            ring_copy(q, d).wait_recv()
            t = 2 + 2 * r + d

            @pl.when(elsewhere(t))
            def _():
                row_copy(t, part(j), jnp.where(side(t) == 0, above, below)).start()

    def dots(t):
        other = elsewhere(t)

        @pl.when(other)
        def _():
            row_copy(t, pl.ds(0, width), above).wait_recv()

        block = blocks[jnp.where(other, 1, 0), t]
        sent[t] = jnp.dot(own[side(t)], block, preferred_element_type=jnp.float32)
        core_copy(t).start()

    def grads(t):
        core_copy(t).wait()
        probs = jax.nn.sigmoid(scale * (sent[t] + got[t]) + offset)
        row = lax.broadcasted_iota(jnp.int32, (rows, rows), 0)
        column = lax.broadcasted_iota(jnp.int32, (rows, rows), 1)
        match = jnp.where(t < 2, 1.0, 0.0)
        probs = probs - jnp.where(row == column, match, 0.0)
        weight = (scale * probs).astype(jnp.bfloat16)
        block = blocks[jnp.where(elsewhere(t), 1, 0), t]
        out_ref[side(t)] += lax.dot_general(
            block, weight, (((1,), (1,)), ((), ())), preferred_element_type=jnp.float32
        )

    for q in range(WINDOW):
        for d in range(2):
            ring_copy(q, d).start()

    own[0] = blocks[0, 1].T
    own[1] = blocks[0, 0].T
    scale, offset = scale_ref[0], offset_ref[0]

    @pl.loop(WINDOW, STEPS)
    def _(q):
        for d in range(2):
            ring_copy(q - WINDOW, d).wait_send()
            ring_copy(q, d).start()

        @pl.when(q >= DELAY)
        def _():
            arrive(q - DELAY)

        t = (q - LAG) // EACH

        @pl.when((q >= LAG) & (lax.rem(q - LAG, EACH) == 0))
        def _():
            dots(t)

            @pl.when(t > 0)
            def _():
                grads(t - 1)

    @pl.loop(STEPS - DELAY, STEPS)
    def _(q):
        arrive(q)

    @pl.loop((STEPS - 1 - LAG) // EACH + 1, SLOTS + 1)
    def _(t):
        @pl.when(t < SLOTS)
        def _():
            dots(t)

        grads(t - 1)

    for q in range(STEPS - WINDOW, STEPS):
        for d in range(2):
            ring_copy(q, d).wait_send()

    @pl.loop(2, SLOTS)
    def _(t):
        @pl.when(elsewhere(t))
        def _():
            row_copy(t, pl.ds(0, width), above).wait_send()


def on_device(n, picture_embeddings, description_embeddings, sharpness_factor, offset_term):
    rows, width = picture_embeddings.shape
    hbm = pl.BlockSpec(memory_space=pl.ANY)
    vmem = pl.BlockSpec(memory_space=pltpu.VMEM)
    smem = pl.BlockSpec(memory_space=pltpu.SMEM)
    grads = pl.pallas_call(
        functools.partial(kernel, n),
        out_shape=jax.ShapeDtypeStruct((2, width, rows), jnp.float32),
        in_specs=[smem, smem, hbm, hbm],
        out_specs=vmem,
        scratch_shapes=[
            pltpu.VMEM((2, SLOTS, width, rows), jnp.bfloat16),
            pltpu.VMEM((2, rows, width), jnp.bfloat16),
            pltpu.VMEM((SLOTS, rows, rows), jnp.float32),
            pltpu.VMEM((SLOTS, rows, rows), jnp.float32),
            pltpu.SemaphoreType.DMA((2,)),
            pltpu.SemaphoreType.DMA((2, WINDOW)),
            pltpu.SemaphoreType.DMA((SLOTS, PIECES)),
            pltpu.SemaphoreType.DMA((SLOTS,)),
            pltpu.SemaphoreType.DMA((SLOTS,)),
            pltpu.SemaphoreType.DMA((SLOTS,)),
            pltpu.SemaphoreType.DMA((SLOTS,)),
        ],
        compiler_params=pltpu.CompilerParams(
            collective_id=0, has_side_effects=True, vmem_limit_bytes=40 * 1024 * 1024
        ),
    )(sharpness_factor, offset_term, picture_embeddings.T, description_embeddings.T)
    return grads[0].T, grads[1].T


def solution(mesh):
    placed = (P("blk", "grp"), P("blk", "grp"), P(), P())
    return jax.shard_map(
        functools.partial(on_device, mesh.shape["blk"]),
        mesh=mesh,
        in_specs=placed,
        out_specs=(P("blk", "grp"), P("blk", "grp")),
        check_vma=False,
    )
```

time: 81.2 us -> 78.6 us (0.968)
  the two profiles are of different devices: /device:TPU:65 before, /device:TPU:1 now
where the time goes in v2:
time: 78.6 us; the launch traced here: 78.4 us
  Pallas kernels  73.4 us (93%)
  local copies, waits for them, and re-layouts  3 us (4%)
  between operations  1.94 us (2%)
    pallas_call x1, Pallas kernels, on_device(): pl.pallas_call(functools.partial(kernel, n), out_shape=jax.ShapeDtypeStru...  73.4 us
    unnamed x4, local copies, waits for them, and re-layouts  1.92 us

profile of v2, /device:TPU:1, one launch (start us, length us, event | category | flops | bytes accessed | tf_op | source)
XLA Modules:
  0.0 78.4 jit_solution(580672473932829441)
XLA Ops:
  1.9 0.0 copy-start
  1.9 1.0 %copy-done = bf16[256,576]{0,1:T(8,128)(2,1)S(1)} copy-done((bf16[256,576]{0,1:T(8,128)(2,1)S(1)}, bf16[256,576]{0,1:T(8,128)(2,1)}, u32[]{:S(2)}) %copy-start) | copy-done | bytes 294936
  2.9 0.0 copy-start.1
  2.9 1.0 %copy-done.1 = bf16[256,576]{0,1:T(8,128)(2,1)S(1)} copy-done((bf16[256,576]{0,1:T(8,128)(2,1)S(1)}, bf16[256,576]{0,1:T(8,128)(2,1)}, u32[]{:S(2)}) %copy-start.1) | copy-done | bytes 294936
  3.8 73.4 %shard_map.59 = f32[2,576,256]{2,1,0:T(8,128)S(1)} custom-call(f32[1]{0:T(128)S(6)} %copy.6.scale_ref, f32[1]{0:T(128)S(6)} %copy.7.offset_ref, bf16[576,256]{1,0:T(8,128)(2,1)S(1)} %bitcast.10, bf16[576,256]{1,0:T(8,128)(2,1)S(1)} %bitcast.11), custom_call_target="tpu_custom_call" | custom-call | tf_op jit(solution)/shard_map/pallas_call | solution.py:200
  77.3 1.1 %slice_bitcast_fusion = (f32[256,576]{0,1:T(8,128)}, f32[256,576]{0,1:T(8,128)}) fusion(f32[2,576,256]{2,1,0:T(8,128)S(1)} %shard_map.59), kind=kLoop, calls=%fused_computation | loop fusion | bytes 2359296 | tf_op jit(solution)/shard_map/transpose | solution.py:222
Async XLA Ops:
  1.9 1.0 %copy-start = (bf16[256,576]{0,1:T(8,128)(2,1)S(1)}, bf16[256,576]{0,1:T(8,128)(2,1)}, u32[]{:S(2)}) copy-start(bf16[256,576]{0,1:T(8,128)(2,1)} %param.4) | copy-start | bytes 884740
  2.9 1.0 %copy-start.1 = (bf16[256,576]{0,1:T(8,128)(2,1)S(1)}, bf16[256,576]{0,1:T(8,128)(2,1)}, u32[]{:S(2)}) copy-start(bf16[256,576]{0,1:T(8,128)(2,1)} %param.5) | copy-start | bytes 884740

commit v3 on v2

--- a/solution.py
+++ b/solution.py
@@ -11,8 +11,9 @@
 PIECES = 4
 WINDOW = 4
 DELAY = 4
-LAG = 5
-EACH = PIECES // 2
+LAG = 19
+HELD = 7
+LAYERS = 12
 SLOTS = 2 * HOPS
 STEPS = (HOPS - 1) * PIECES
 MESH = pl.DeviceIdType.MESH
@@ -34,6 +35,7 @@
     recv_sem,
     row_send_sem,
     row_recv_sem,
+    ready_sem,
     core_send_sem,
     core_recv_sem,
 ):
@@ -47,6 +49,8 @@
     behind = start + lax.rem(place + HOPS - 1, HOPS)
     above, below = lax.rem(me + HOPS, n), lax.rem(me + n - HOPS, n)
     partner = (me, 1 - core)
+    first = lax.rem(me // HOPS, LAYERS) == 0
+    held = jnp.where(first, HELD, 0)
 
     loads = [
         pltpu.make_async_copy(text_ref, blocks.at[0, 0], load_sem.at[0]),
@@ -55,13 +59,14 @@
     for load in loads:
         load.start()
     barrier = pltpu.get_barrier_semaphore()
-    others = [(ahead, core), (behind, core), (above, core), (below, core), partner]
+    others = [(ahead, core), (behind, core), (below, core), partner]
     for other in others:
         pl.semaphore_signal(barrier, inc=1, device_id=other, device_id_type=MESH)
     out_ref[...] = jnp.zeros_like(out_ref)
     for load in loads:
         load.wait()
     pl.semaphore_wait(barrier, len(others))
+    pl.semaphore_signal(ready_sem, inc=1, device_id=(above, core), device_id_type=MESH)
 
     def part(j):
         return pl.ds(pl.multiple_of(j * piece, 16), piece)
@@ -107,15 +112,42 @@
             device_id_type=MESH,
         )
 
+    def pass_down(q, d):
+        r, j = q // PIECES, lax.rem(q, PIECES)
+        t = 2 + 2 * r + d
+
+        @pl.when(elsewhere(t) & (side(t) == 1))
+        def _():
+            row_copy(t, part(j), below).start()
+
     def arrive(q):
         r, j = q // PIECES, lax.rem(q, PIECES)
+
+        @pl.when(q == held)
+        def _():
+            pl.semaphore_wait(ready_sem, 1)
+
+            @pl.when(first)
+            def _():
+                @pl.loop(0, HELD)
+                def _(past):
+                    for d in range(2):
+                        pass_down(past, d)
+
         for d in range(2):
             ring_copy(q, d).wait_recv()
             t = 2 + 2 * r + d
 
-            @pl.when(elsewhere(t))
+            @pl.when(elsewhere(t) & (side(t) == 0))
             def _():
-                row_copy(t, part(j), jnp.where(side(t) == 0, above, below)).start()
+                row_copy(t, part(j), above).start()
+
+            @pl.when(q >= held)
+            def _():
+                pass_down(q, d)
+
+    def put_off(t):
+        return first & elsewhere(t) & (side(t) == 0)
 
     def dots(t):
         other = elsewhere(t)
@@ -141,6 +173,15 @@
             block, weight, (((1,), (1,)), ((), ())), preferred_element_type=jnp.float32
         )
 
+    def products(t, apart, chosen):
+        @pl.when((t < SLOTS) & chosen(t))
+        def _():
+            dots(t)
+
+        @pl.when((t >= apart) & chosen(t - apart))
+        def _():
+            grads(t - apart)
+
     for q in range(WINDOW):
         for d in range(2):
             ring_copy(q, d).start()
@@ -149,37 +190,31 @@
     own[1] = blocks[0, 0].T
     scale, offset = scale_ref[0], offset_ref[0]
 
-    @pl.loop(WINDOW, STEPS)
+    @pl.loop(WINDOW, STEPS + DELAY)
     def _(q):
-        for d in range(2):
-            ring_copy(q - WINDOW, d).wait_send()
-            ring_copy(q, d).start()
+        @pl.when(q < STEPS)
+        def _():
+            for d in range(2):
+                ring_copy(q - WINDOW, d).wait_send()
+                ring_copy(q, d).start()
 
         @pl.when(q >= DELAY)
         def _():
             arrive(q - DELAY)
 
-        t = (q - LAG) // EACH
-
-        @pl.when((q >= LAG) & (lax.rem(q - LAG, EACH) == 0))
-        def _():
-            dots(t)
-
-            @pl.when(t > 0)
-            def _():
-                grads(t - 1)
-
-    @pl.loop(STEPS - DELAY, STEPS)
-    def _(q):
-        arrive(q)
-
-    @pl.loop((STEPS - 1 - LAG) // EACH + 1, SLOTS + 1)
+        @pl.when(q >= LAG)
+        def _():
+            products(q - LAG, 1, lambda t: ~put_off(t))
+
+    @pl.loop(STEPS + DELAY - LAG, SLOTS + 1)
     def _(t):
-        @pl.when(t < SLOTS)
-        def _():
-            dots(t)
-
-        grads(t - 1)
+        products(t, 1, lambda t: ~put_off(t))
+
+    @pl.when(first)
+    def _():
+        @pl.loop(2, SLOTS + 4)
+        def _(t):
+            products(t, 4, put_off)
 
     for q in range(STEPS - WINDOW, STEPS):
         for d in range(2):
@@ -212,6 +247,7 @@
             pltpu.SemaphoreType.DMA((SLOTS, PIECES)),
             pltpu.SemaphoreType.DMA((SLOTS,)),
             pltpu.SemaphoreType.DMA((SLOTS,)),
+            pltpu.SemaphoreType.REGULAR,
             pltpu.SemaphoreType.DMA((SLOTS,)),
             pltpu.SemaphoreType.DMA((SLOTS,)),
         ],

time: 78.6 us -> 78.5 us (level)
  no operation moved by 1% of the time
where the time goes in v3:
time: 78.5 us; the launch traced here: 78.3 us
  Pallas kernels  73.4 us (94%)
  local copies, waits for them, and re-layouts  3 us (4%)
  between operations  1.94 us (2%)
    pallas_call x1, Pallas kernels, on_device(): pl.pallas_call(functools.partial(kernel, n), out_shape=jax.ShapeDtypeStru...  73.4 us
    unnamed x4, local copies, waits for them, and re-layouts  1.92 us

profile of v3, /device:TPU:1, one launch (start us, length us, event | category | flops | bytes accessed | tf_op | source)
XLA Modules:
  0.0 78.3 jit_solution(17390782447836232048)
XLA Ops:
  1.9 0.0 copy-start
  1.9 1.0 %copy-done = bf16[256,576]{0,1:T(8,128)(2,1)S(1)} copy-done((bf16[256,576]{0,1:T(8,128)(2,1)S(1)}, bf16[256,576]{0,1:T(8,128)(2,1)}, u32[]{:S(2)}) %copy-start) | copy-done | bytes 294936
  2.9 0.0 copy-start.1
  2.9 1.0 %copy-done.1 = bf16[256,576]{0,1:T(8,128)(2,1)S(1)} copy-done((bf16[256,576]{0,1:T(8,128)(2,1)S(1)}, bf16[256,576]{0,1:T(8,128)(2,1)}, u32[]{:S(2)}) %copy-start.1) | copy-done | bytes 294936
  3.8 73.4 %shard_map.59 = f32[2,576,256]{2,1,0:T(8,128)S(1)} custom-call(f32[1]{0:T(128)S(6)} %copy.6.scale_ref, f32[1]{0:T(128)S(6)} %copy.7.offset_ref, bf16[576,256]{1,0:T(8,128)(2,1)S(1)} %bitcast.10, bf16[576,256]{1,0:T(8,128)(2,1)S(1)} %bitcast.11), custom_call_target="tpu_custom_call" | custom-call | tf_op jit(solution)/shard_map/pallas_call | solution.py:235
  77.2 1.1 %slice_bitcast_fusion = (f32[256,576]{0,1:T(8,128)}, f32[256,576]{0,1:T(8,128)}) fusion(f32[2,576,256]{2,1,0:T(8,128)S(1)} %shard_map.59), kind=kLoop, calls=%fused_computation | loop fusion | bytes 2359296 | tf_op jit(solution)/shard_map/transpose | solution.py:258
Async XLA Ops:
  1.9 1.0 %copy-start = (bf16[256,576]{0,1:T(8,128)(2,1)S(1)}, bf16[256,576]{0,1:T(8,128)(2,1)}, u32[]{:S(2)}) copy-start(bf16[256,576]{0,1:T(8,128)(2,1)} %param.4) | copy-start | bytes 884740
  2.9 1.0 %copy-start.1 = (bf16[256,576]{0,1:T(8,128)(2,1)S(1)}, bf16[256,576]{0,1:T(8,128)(2,1)}, u32[]{:S(2)}) copy-start(bf16[256,576]{0,1:T(8,128)(2,1)} %param.5) | copy-start | bytes 884740

commit v4 on v3

--- a/solution.py
+++ b/solution.py
@@ -9,8 +9,8 @@
 
 HOPS = 8
 PIECES = 4
-WINDOW = 4
-DELAY = 4
+WINDOW = 3
+DELAY = 3
 LAG = 19
 HELD = 7
 LAYERS = 12
@@ -71,11 +71,17 @@
     def part(j):
         return pl.ds(pl.multiple_of(j * piece, 16), piece)
 
+    def source(r, d):
+        t = 2 + 2 * r + d
+        if d:
+            return jnp.where(r < 2, 1 - r, t - 4)
+        return jnp.where(r == 0, 0, jnp.where(r == 1, 2, jnp.where(r == 2, 1, t - 4)))
+
     def ring_copy(q, d):
         r, j = q // PIECES, lax.rem(q, PIECES)
         t = 2 + 2 * r + d
         return pltpu.make_async_remote_copy(
-            src_ref=blocks.at[0, jnp.where(r < 2, lax.rem(r + d, 2), t - 4), part(j)],
+            src_ref=blocks.at[0, source(r, d), part(j)],
             dst_ref=blocks.at[0, t, part(j)],
             send_sem=send_sem.at[d, lax.rem(q, WINDOW)],
             recv_sem=recv_sem.at[t, j],
@@ -95,12 +101,15 @@
 
     def elsewhere(t):
         r, d = t // 2 - 1, lax.rem(t, 2)
-        s = r // 2
+        caption = side(t) == 0
+        s = jnp.where(d == 1, r // 2, jnp.where(caption, (r + 1) // 2, r // 2 - 1))
         wrapped = jnp.where(d == 0, place - 1 - s < 0, place + 1 + s >= HOPS)
-        return (t >= 2) & (wrapped == (lax.rem(r, 2) == 0))
+        return (t >= 2) & (wrapped == ((d == 0) == caption))
 
     def side(t):
-        return jnp.where(t < 2, t, lax.rem(t // 2 + 1 + lax.rem(t, 2), 2))
+        r, d = t // 2 - 1, lax.rem(t, 2)
+        image = jnp.where((d == 0) & (r == 0), 0, 1 - lax.rem(r, 2))
+        return jnp.where(t < 2, t, image)
 
     def core_copy(t):
         return pltpu.make_async_remote_copy(

time: 78.5 us -> 78 us (level)
  no operation moved by 1% of the time
where the time goes in v4:
time: 78 us; the launch traced here: 77.7 us
  Pallas kernels  72.8 us (93%)
  local copies, waits for them, and re-layouts  3 us (4%)
  between operations  1.94 us (2%)
    pallas_call x1, Pallas kernels, on_device(): pl.pallas_call(functools.partial(kernel, n), out_shape=jax.ShapeDtypeStru...  72.8 us
    unnamed x4, local copies, waits for them, and re-layouts  1.92 us

profile of v4, /device:TPU:1, one launch (start us, length us, event | category | flops | bytes accessed | tf_op | source)
XLA Modules:
  0.0 77.7 jit_solution(8480592145459341272)
XLA Ops:
  1.9 0.0 copy-start
  1.9 1.0 %copy-done = bf16[256,576]{0,1:T(8,128)(2,1)S(1)} copy-done((bf16[256,576]{0,1:T(8,128)(2,1)S(1)}, bf16[256,576]{0,1:T(8,128)(2,1)}, u32[]{:S(2)}) %copy-start) | copy-done | bytes 294936
  2.9 0.0 copy-start.1
  2.9 1.0 %copy-done.1 = bf16[256,576]{0,1:T(8,128)(2,1)S(1)} copy-done((bf16[256,576]{0,1:T(8,128)(2,1)S(1)}, bf16[256,576]{0,1:T(8,128)(2,1)}, u32[]{:S(2)}) %copy-start.1) | copy-done | bytes 294936
  3.8 72.8 %shard_map.59 = f32[2,576,256]{2,1,0:T(8,128)S(1)} custom-call(f32[1]{0:T(128)S(6)} %copy.6.scale_ref, f32[1]{0:T(128)S(6)} %copy.7.offset_ref, bf16[576,256]{1,0:T(8,128)(2,1)S(1)} %bitcast.10, bf16[576,256]{1,0:T(8,128)(2,1)S(1)} %bitcast.11), custom_call_target="tpu_custom_call" | custom-call | tf_op jit(solution)/shard_map/pallas_call | solution.py:244
  76.6 1.1 %slice_bitcast_fusion = (f32[256,576]{0,1:T(8,128)}, f32[256,576]{0,1:T(8,128)}) fusion(f32[2,576,256]{2,1,0:T(8,128)S(1)} %shard_map.59), kind=kLoop, calls=%fused_computation | loop fusion | bytes 2359296 | tf_op jit(solution)/shard_map/transpose | solution.py:267
Async XLA Ops:
  1.9 1.0 %copy-start = (bf16[256,576]{0,1:T(8,128)(2,1)S(1)}, bf16[256,576]{0,1:T(8,128)(2,1)}, u32[]{:S(2)}) copy-start(bf16[256,576]{0,1:T(8,128)(2,1)} %param.4) | copy-start | bytes 884740
  2.9 1.0 %copy-start.1 = (bf16[256,576]{0,1:T(8,128)(2,1)S(1)}, bf16[256,576]{0,1:T(8,128)(2,1)}, u32[]{:S(2)}) copy-start(bf16[256,576]{0,1:T(8,128)(2,1)} %param.5) | copy-start | bytes 884740
